TPU v7x, 32 devices: a whole 2x2x4 slice. The times are simulated.
32 devices in a mesh: groups: 2 (over y), branch: 4 (over z), rhs: 2 (over x), inner: 2 (over core).
Axes of the slice: x: 2, y: 2, z: 4, core: 2. Of those that a mesh axis runs over, the one named last changes fastest.
Arguments:
- vectors: float32 [32, 16384], P('rhs', ('groups', 'branch', 'inner')), parts along dimension 1, may hold values from -6 to 6
- leaf_basis: float32 [64, 16384], P(None, ('groups', 'branch', 'inner')), parts along dimension 1, may hold values from -0.75 to 0.75
- near_blocks: float32 [3, 64, 16384], P(None, None, ('groups', 'branch', 'inner')), parts along dimension 2, may hold values from -0.4375 to 0.4375
- transfer: float32 [64, 31744], P(None, ('groups', 'branch', 'inner')), parts along dimension 1, may hold values from -0.5 to 0.5
- coupling: float32 [64, 63488], P(None, ('groups', 'branch', 'inner')), parts along dimension 1, may hold values from -0.5 to 0.5
- coupling_source: int32 [496, 2], P(('groups', 'branch', 'inner')), parts along dimension 0, may hold values from 0 to 127, as said below
- top_transfer: float32 [64, 512], P(None, 'groups'), parts along dimension 1, may hold values from -0.5 to 0.5
- upper_coupling_matrices: float32 [64, 2048], P(None, ('groups', 'branch')), parts along dimension 1, may hold values from -0.5 to 0.5
- top_target: int32 [32], P(('groups', 'branch')), parts along dimension 0, may hold values from 0 to 5, as said below
- top_source: int32 [32], P(('groups', 'branch')), parts along dimension 0, may hold values from 0 to 5, as said below
Outputs:
- product: float32 [32, 16384], P('rhs', ('groups', 'branch', 'inner')), parts along dimension 1
There are 2 independent parts, one for each index of `groups`. A program takes and returns all parts, laid end to end along the dimension named above; each array names one. Nothing has to cross between parts.
Inputs may be any that keep to these rules, and one draw needn't show every extreme that they name: `coupling_source`: the partner of lower cluster c of a level with w = 16 / 2^h clusters per run lies in the same run of w clusters as c or in the run just before or after it (runs are c div w); a run at either end has no run beyond it. `top_target`: pairs alternate in level: even pairs join two different branch clusters (ids below 4), odd pairs two different clusters of the next level (ids 4 and above). `top_source`: same level as the pair's target and never equal to it.
All inputs are finite; a program needn't handle non-finite values.
Results may differ from a plain program's by a relative error of at most 0.0001.
Values sent between devices are 32-bit elements; how exact they have to be, the bound alone decides.
A program may use at most 64 MiB of HBM per device.

v0:
```python
import jax
import jax.numpy as jnp
import numpy as np
from jax import lax
from jax.sharding import PartitionSpec as P

EXACT = lax.Precision.HIGHEST


def with_halo(block, sides, width):
    for axis, dim in sides:
        count = lax.axis_size(axis)
        forward = [(i, i + 1) for i in range(count - 1)]
        backward = [(target, source) for source, target in forward]
        low = lax.ppermute(
            lax.slice_in_dim(block, block.shape[dim] - width, None, axis=dim), axis, forward
        )
        high = lax.ppermute(lax.slice_in_dim(block, 0, width, axis=dim), axis, backward)
        block = jnp.concatenate([low, block, high], axis=dim)
    return block


def on_device(
    vectors,
    leaf_basis,
    near_blocks,
    transfer,
    coupling,
    coupling_source,
    top_transfer,
    upper_coupling_matrices,
    top_target,
    top_source,
):
    rank_dim = leaf_basis.shape[0]
    leaf_len = near_blocks.shape[1]
    leaves = leaf_basis.shape[1] // leaf_len
    levels = leaves.bit_length() - 1
    clusters = 2 * leaves - 1
    partner_clusters = coupling_source.shape[1]
    columns = vectors.shape[0]
    inner_count = lax.axis_size("inner")
    top_width = top_transfer.shape[1] // rank_dim
    starts = [2 * leaves - 2 * (leaves >> height) for height in range(levels + 1)]
    breadth_table = np.concatenate(
        [np.full((leaves >> height,), leaves >> height, np.int32) for height in range(levels + 1)]
    )
    start_table = np.concatenate(
        [np.full((leaves >> height,), starts[height], np.int32) for height in range(levels + 1)]
    )
    blocks = vectors.reshape(columns, leaves, leaf_len)
    basis_blocks = leaf_basis.reshape(rank_dim, leaves, leaf_len)
    transfers = transfer.reshape(rank_dim, clusters, rank_dim)
    coefs = [jnp.einsum("rti,cti->tcr", basis_blocks, blocks, precision=EXACT)]
    for height in range(levels):
        breadth = leaves >> height
        moving = transfers[:, starts[height] : starts[height] + breadth]
        lifted = jnp.einsum("aqb,qca->qcb", moving, coefs[height], precision=EXACT)
        coefs.append(lifted.reshape(breadth // 2, 2, columns, rank_dim).sum(1))
    root_move = transfers[:, clusters - 1]
    root_term = jnp.dot(coefs[levels][0], root_move, precision=EXACT)
    coef_table = jnp.concatenate(coefs + [root_term[None]], axis=0)
    stride = clusters + 1
    breadth_col = jnp.asarray(breadth_table)[:, None]
    source_dev = coupling_source // breadth_col
    source_pos = coupling_source % breadth_col + jnp.asarray(start_table)[:, None]
    gathered = lax.all_gather(coef_table, ("branch", "inner"), axis=0, tiled=True)
    row_ids = source_dev * stride + source_pos
    root_rows = gathered.reshape(-1, stride, columns, rank_dim)[:, clusters]
    picked = jnp.take(gathered, row_ids.reshape(-1), axis=0)
    slot_blocks = coupling.reshape(rank_dim, clusters * partner_clusters, rank_dim)
    coupled = jnp.einsum("aqb,qcb->qca", slot_blocks, picked, precision=EXACT)
    coupled = coupled.reshape(clusters, partner_clusters, columns, rank_dim).sum(1)
    leading_upper_index = root_rows.reshape(top_width, inner_count, columns, rank_dim).sum(1)
    top_moves = top_transfer.reshape(rank_dim, top_width, rank_dim)
    second = jnp.einsum("aqb,qca->qcb", top_moves, leading_upper_index, precision=EXACT)
    second = second.reshape(top_width // 2, 2, columns, rank_dim).sum(1)
    top_coef = jnp.concatenate([leading_upper_index, second], axis=0)
    chosen = jnp.take(top_coef, top_source, axis=0)
    slot_terms = jnp.einsum(
        "aqb,qcb->qca",
        upper_coupling_matrices.reshape(rank_dim, -1, rank_dim),
        chosen,
        precision=EXACT,
    )
    selector = (
        top_target[None, :] == jnp.arange(top_width + top_width // 2, dtype=jnp.int32)[:, None]
    ).astype(jnp.float32)
    partial_top = jnp.einsum("kq,qca->kca", selector, slot_terms, precision=EXACT)
    top_field = lax.psum(partial_top, "branch")
    field_first = top_field[:top_width] + jnp.einsum(
        "aqb,qcb->qca", top_moves, jnp.repeat(top_field[top_width:], 2, axis=0), precision=EXACT
    )
    own_field = lax.dynamic_index_in_dim(field_first, lax.axis_index("branch"), 0, keepdims=False)
    root_cluster_state = jnp.dot(own_field, root_move.T, precision=EXACT)
    fields = coupled[clusters - 1 :] + root_cluster_state[None]
    for height in reversed(range(levels)):
        breadth = leaves >> height
        moving = transfers[:, starts[height] : starts[height] + breadth]
        fields = coupled[starts[height] : starts[height] + breadth] + jnp.einsum(
            "aqb,qcb->qca", moving, jnp.repeat(fields, 2, axis=0), precision=EXACT
        )
    result = jnp.einsum("rti,tcr->cti", basis_blocks, fields, precision=EXACT)
    padded = with_halo(vectors, ((("branch", "inner"), 1),), leaf_len)
    extended = padded.reshape(columns, leaves + 2, leaf_len)
    stencil = near_blocks.reshape(3, leaf_len, leaves, leaf_len)
    for offset in range(3):
        result = result + jnp.einsum(
            "jti,ctj->cti", stencil[offset], extended[:, offset : offset + leaves], precision=EXACT
        )
    return result.reshape(columns, leaves * leaf_len)


def solution(mesh):
    placed = (
        P("rhs", ("groups", "branch", "inner")),
        P(None, ("groups", "branch", "inner")),
        P(None, None, ("groups", "branch", "inner")),
        P(None, ("groups", "branch", "inner")),
        P(None, ("groups", "branch", "inner")),
        P(("groups", "branch", "inner"), None),
        P(None, "groups"),
        P(None, ("groups", "branch")),
        P(("groups", "branch")),
        P(("groups", "branch")),
    )
    return jax.shard_map(
        on_device,
        mesh=mesh,
        in_specs=placed,
        out_specs=P("rhs", ("groups", "branch", "inner")),
        check_vma=False,
    )
```

profile of v0, /device:TPU:0, one launch (start us, length us, event | category | flops | bytes accessed | tf_op | source)
XLA Modules:
  0.0 99.8 jit_solution(3012436344236489321)
XLA Ops:
  6.5 1.5 %reshape.125 = f32[64,31,64]{2,1,0:T(8,128)S(1)} reshape(f32[64,1984]{1,0:T(8,128)} %param.15) | data formatting | bytes 1015808 | tf_op jit(solution)/shard_map/reshape | solution.py:53
  8.4 1.2 %reshape.124 = f32[64,16,64]{2,1,0:T(8,128)S(1)} reshape(f32[64,1024]{1,0:T(8,128)} %param.13) | data formatting | bytes 524288 | tf_op jit(solution)/shard_map/reshape | solution.py:52
  9.7 1.1 %constant_dynamic-update-slice_fusion.4 = (f32[32,16,64]{2,1,0:T(8,128)S(1)}, f32[16,16,64]{2,1,0:T(8,128)S(1)}) fusion(f32[64,16,64]{2,1,0:T(8,128)S(1)} %reshape.124, f32[16,16,64]{2,1,0:T(8,128)S(1)} %reshape.123), kind=kOutput, calls=%fused_computation.64 | convolution fusion | flops 12582911 | bytes 589824 | tf_op jit(solution)/shard_map/rti,cti->tcr/dot_general | solution.py:54
  10.8 0.7 bitcast_reduce_fusion
  11.5 0.4 bitcast_reduce_fusion.2
  11.8 0.2 bitcast_reduce_fusion.4
  12.5 0.7 copy-done.4
  13.2 0.7 fusion.55
  13.9 2.3 %collective-permute-start = (f32[16,64]{1,0:T(8,128)}, f32[16,64]{1,0:T(8,128)S(1)}, u32[]{:S(2)}, u32[]{:S(2)}) collective-permute-start(f32[16,64]{1,0:T(8,128)} %get-tuple-element.12), channel_id=1, source_target_pairs={{0,1},{1,4},{4,5},{5,8},{8,9},{9,12},{12,13},{2,3},{3,6},{6,7},{7,... | collective-permute-start | bytes 12296 | tf_op jit(solution)/shard_map/ppermute | solution.py:15
  16.2 1.3 %collective-permute-start.1 = (f32[16,64]{1,0:T(8,128)}, f32[16,64]{1,0:T(8,128)S(1)}, u32[]{:S(2)}, u32[]{:S(2)}) collective-permute-start(f32[16,64]{1,0:T(8,128)} %get-tuple-element.11), channel_id=1, source_target_pairs={{1,0},{4,1},{5,4},{8,5},{9,8},{12,9},{13,12},{3,2},{6,3},{7,6},{10... | collective-permute-start | bytes 12296 | tf_op jit(solution)/shard_map/ppermute | solution.py:18
  18.0 0.6 pad_clamp_fusion
  18.6 0.5 compare_and_fusion
  19.1 0.6 compare_and_fusion.1
  19.7 0.9 fusion.53
  20.6 0.6 pad_clamp_fusion.1
  21.2 0.7 reshape.133
  21.9 0.8 reshape.135
  22.7 2.1 %reshape.130 = f32[64,62,64]{2,1,0:T(8,128)S(1)} reshape(f32[64,3968]{1,0:T(8,128)} %param.16) | data formatting | bytes 2031616 | tf_op jit(solution)/shard_map/reshape | solution.py:71
  24.8 1.9 %squeeze.19 = f32[64,16,64]{2,1,0:T(8,128)} reshape(f32[1,64,1024]{2,1,0:T(8,128)} %get-tuple-element.6) | data formatting | bytes 524288 | tf_op jit(solution)/shard_map/squeeze | solution.py:109
  26.7 1.9 %squeeze.20 = f32[64,16,64]{2,1,0:T(8,128)} reshape(f32[1,64,1024]{2,1,0:T(8,128)} %get-tuple-element.7) | data formatting | bytes 524288 | tf_op jit(solution)/shard_map/squeeze | solution.py:109
  28.6 1.9 %squeeze.21 = f32[64,16,64]{2,1,0:T(8,128)} reshape(f32[1,64,1024]{2,1,0:T(8,128)} %get-tuple-element.5) | data formatting | bytes 524288 | tf_op jit(solution)/shard_map/squeeze | solution.py:109
  30.5 1.6 %concatenate.11 = f32[16,1152]{1,0:T(8,128)} concatenate(f32[16,64]{1,0:T(8,128)S(1)} %collective-permute-done, f32[16,1024]{1,0:T(8,128)} %param.12, f32[16,64]{1,0:T(8,128)S(1)} %collective-permute-done.1), dimensions={1} | concatenate | bytes 147456 | tf_op jit(solution)/shard_map/concatenate | solution.py:19
  32.1 1.6 %reshape.141 = f32[16,18,64]{2,1,0:T(8,128)} reshape(f32[16,1152]{1,0:T(8,128)} %concatenate.11) | data formatting | bytes 147456 | tf_op jit(solution)/shard_map/reshape | solution.py:105
  33.7 2.0 %fusion.54 = (f32[16,16,64]{2,1,0:T(8,128)}, f32[16,16,64]{2,1,0:T(8,128)}, f32[16,16,64]{2,1,0:T(8,128)}) fusion(f32[16,18,64]{2,1,0:T(8,128)} %reshape.141), kind=kLoop, calls=%fused_computation.87 | loop fusion | bytes 393216 | tf_op jit(solution)/shard_map/slice | solution.py:109
  35.7 9.5 %all-gather.2.cloned.1.call-done = f32[256,16,64]{2,1,0:T(8,128)} async-done(((f32[32,16,64]{2,1,0:T(8,128)}), f32[256,16,64]{2,1,0:T(8,128)}) %all-gather.2.cloned.1.call-update) | async-done | bytes 1048592 | tf_op jit(solution)/shard_map/all_gather | solution.py:67
  45.1 0.8 slice.105
  46.0 1.1 %bitcast_reduce_fusion.3 = f32[2,16,64]{2,1,0:T(8,128)S(1)} fusion(f32[4,16,64]{2,1,0:T(8,128)S(1)} %bitcast_reduce_fusion.1, f32[64,4,64]{2,1,0:T(4,128)} %reshape.133), kind=kOutput, calls=%fused_computation.53 | convolution fusion | flops 3147776 | bytes 90112 | tf_op jit(solution)/shard_map/aqb,qca->qcb/dot_general | solution.py:76
  47.1 0.6 pad_maximum_fusion
  47.8 2.1 %gather_fusion.1 = f32[4,16,64]{2,1,0:T(8,128)} fusion(f32[6,16,64]{2,1,0:T(8,128)} %pad_maximum_fusion, s32[1024]{0:T(1024)} %pad_clamp_fusion), kind=kCustom, calls=%fused_computation.1 | custom fusion | bytes 32784 | tf_op jit(solution)/shard_map/jit(_take)/gather | solution.py:79
  49.8 1.3 %fusion.25 = f32[4,16,64]{2,1,0:T(8,128)S(1)} fusion(f32[64,4,64]{2,1,0:T(4,128)} %reshape.135, f32[4,16,64]{2,1,0:T(8,128)} %gather_fusion.1, pred[4]{0:T(512)(128)(4,1)} %compare_and_fusion), kind=kOutput, calls=%fused_computation.37 | convolution fusion | flops 3149824 | bytes 98308 | tf_op jit(solution)/shard_map/aqb,qcb->qca/dot_general | solution.py:80
  51.1 1.6 %fusion.38 = f32[6,16,64]{2,0,1:T(8,128)} fusion(f32[4,16,64]{2,1,0:T(8,128)S(1)} %fusion.25, s32[4]{0:T(128)} %param.20), kind=kOutput, calls=%fused_computation.55 | convolution fusion | flops 294936 | bytes 40976 | tf_op jit(solution)/shard_map/kq,qca->kca/dot_general | solution.py:89
  52.7 19.3 %psum.7 = f32[6,16,64]{2,0,1:T(8,128)} all-reduce(f32[6,16,64]{2,0,1:T(8,128)} %fusion.38), channel_id=1, replica_groups=mesh['groups'=2,'branch'=4,'rhs'=2,'inner'=2] {'branch'}, use_global_device_ids=true, to_apply=%region_6.7 | all-reduce | flops 6144 | bytes 49152 | tf_op jit(solution)/shard_map/psum | solution.py:90
  72.0 0.8 slice.107
  72.9 0.8 slice.106
  73.7 1.2 %fusion.31 = f32[4,16,64]{2,1,0:T(8,128)S(1)} fusion(f32[4,16,64]{2,1,0:T(8,128)S(1)} %bitcast.64, f32[64,4,64]{2,1,0:T(4,128)} %reshape.133), kind=kOutput, calls=%fused_computation.43 | convolution fusion | flops 3145728 | bytes 98304 | tf_op jit(solution)/shard_map/aqb,qcb->qca/dot_general | solution.py:91
  75.0 3.1 %gather_fusion = f32[62,16,64]{2,1,0:T(8,128)} fusion(f32[256,16,64]{2,1,0:T(8,128)} %all-gather.2.cloned.1.call-done, s32[1024]{0:T(1024)} %pad_clamp_fusion.1), kind=kCustom, calls=%fused_computation | custom fusion | bytes 508152 | tf_op jit(solution)/shard_map/jit(_take)/gather | solution.py:70
  78.1 6.0 %fusion = f32[62,16,64]{2,1,0:T(8,128)} fusion(f32[64,62,64]{2,1,0:T(8,128)S(1)} %reshape.130, f32[62,16,64]{2,1,0:T(8,128)} %gather_fusion, pred[62]{0:T(512)(128)(4,1)S(1)} %copy-done.14), kind=kOutput, calls=%fused_computation.2 | convolution fusion | flops 48822272 | bytes 1523774 | tf_op jit(solution)/shard_map/aqb,qcb->qca/dot_general | solution.py:72
  84.1 1.2 %reduce_sum.64 = f32[31,16,64]{2,1,0:T(8,128)S(1)} reduce(f32[31,2,16,64]{3,2,1,0:T(8,128)} %bitcast.56, f32[]{:T(128)} %constant.54.clone.1), dimensions={1}, to_apply=%region_3.0 | reduce | flops 31744 | bytes 380932 | tf_op jit(solution)/shard_map/reduce_sum | solution.py:73
  85.3 1.0 fusion.4
  86.2 1.1 %convolution_add_fusion.6 = f32[2,16,64]{2,1,0:T(8,128)S(1)} fusion(f32[64,2,64]{2,1,0:T(2,128)} %copy-done.5, f32[31,16,64]{2,1,0:T(8,128)S(1)} %reduce_sum.64, f32[16,64]{1,0:T(8,128)S(1)} %fusion.4), kind=kOutput, calls=%fused_computation.11 | convolution fusion | flops 1574912 | bytes 53248 | tf_op jit(solution)/shard_map/aqb,qcb->qca/dot_general | solution.py:100
  87.3 0.3 convolution_add_fusion.5
  87.7 0.5 convolution_add_fusion.4
  88.2 1.0 %convolution_add_fusion.3 = f32[16,16,64]{2,1,0:T(8,128)S(1)} fusion(f32[16,16,64]{2,1,0:T(8,128)S(1)} %bitcast.57, f32[64,16,64]{2,1,0:T(8,128)S(1)} %slice.95, f32[31,16,64]{2,1,0:T(8,128)S(1)} %reduce_sum.64), kind=kOutput, calls=%fused_computation.8 | convolution fusion | flops 12599296 | bytes 458752 | tf_op jit(solution)/shard_map/aqb,qcb->qca/dot_general | solution.py:100
  89.2 0.7 fusion.13
  90.0 0.7 convolution_add_fusion.2
  90.7 0.7 convolution_add_fusion.1
  91.5 0.7 fusion.2
  92.2 0.7 reshape.142
  (65 shorter events, 1.3 us)
Async XLA Ops:
  6.5 3.1 %copy-start.9 = (f32[16,1024]{1,0:T(8,128)S(1)}, f32[16,1024]{1,0:T(8,128)}, u32[]{:S(2)}) copy-start(f32[16,1024]{1,0:T(8,128)} %param.12) | copy-start | bytes 196612
  6.5 38.6 %all-gather.2.cloned.1.call-start = ((), (), s32[]{:S(2)}) async-start(), calls=%async_computation | async-start | bytes 2359296 | tf_op jit(solution)/shard_map/all_gather | solution.py:67
  8.2 9.3 %copy-start.13 = (s32[31,2]{0,1:T(2,128)S(1)}, s32[31,2]{0,1:T(2,128)}, u32[]{:S(2)}) copy-start(s32[31,2]{0,1:T(2,128)} %param.17) | copy-start | bytes 748
  8.2 9.3 %copy-start.15 = (s32[31]{0:T(128)S(1)}, s32[31]{0:T(128)}, u32[]{:S(2)}) copy-start(s32[31]{0:T(128)} %constant.61.clone) | copy-start | bytes 376
  8.2 9.3 %copy-start.16 = (s32[31]{0:T(128)S(1)}, s32[31]{0:T(128)}, u32[]{:S(2)}) copy-start(s32[31]{0:T(128)} %constant.62.clone) | copy-start | bytes 376
  8.3 9.7 %copy-start.17 = (s32[4]{0:T(128)S(1)}, s32[4]{0:T(128)}, u32[]{:S(2)}) copy-start(s32[4]{0:T(128)} %param.21) | copy-start | bytes 52
  8.3 11.4 %copy-start.3 = (f32[3,64,1024]{2,1,0:T(8,128)S(1)}, f32[3,64,1024]{2,1,0:T(8,128)}, u32[]{:S(2)}) copy-start(f32[3,64,1024]{2,1,0:T(8,128)} %param.14) | copy-start | bytes 2359300
  8.3 12.3 %copy-start.5 = (f32[64,2,64]{2,1,0:T(2,128)}, f32[64,2,64]{2,1,0:T(2,128)S(1)}, u32[]{:S(2)}) copy-start(f32[64,2,64]{2,1,0:T(2,128)S(1)} %slice.98) | copy-start | bytes 98308
  8.4 12.2 %copy-start.10 = (f32[64,1,64]{2,1,0:T(1,128)}, f32[64,1,64]{2,1,0:T(1,128)S(1)}, u32[]{:S(2)}) copy-start(f32[64,1,64]{2,1,0:T(1,128)S(1)} %slice.99) | copy-start | bytes 49156
  9.7 11.5 %copy-start.11 = (f32[64,256]{1,0:T(8,128)S(1)}, f32[64,256]{1,0:T(8,128)}, u32[]{:S(2)}) copy-start(f32[64,256]{1,0:T(8,128)} %param.18) | copy-start | bytes 196612
  10.8 11.2 %copy-start.12 = (f32[64,256]{1,0:T(8,128)S(1)}, f32[64,256]{1,0:T(8,128)}, u32[]{:S(2)}) copy-start(f32[64,256]{1,0:T(8,128)} %param.19) | copy-start | bytes 196612
  12.4 0.7 copy-start.4
  13.9 16.7 %collective-permute-start = (f32[16,64]{1,0:T(8,128)}, f32[16,64]{1,0:T(8,128)S(1)}, u32[]{:S(2)}, u32[]{:S(2)}) collective-permute-start(f32[16,64]{1,0:T(8,128)} %get-tuple-element.12), channel_id=1, source_target_pairs={{0,1},{1,4},{4,5},{5,8},{8,9},{9,12},{12,13},{2,3},{3,6},{6,7},{7,... | collective-permute-start | bytes 12296 | tf_op jit(solution)/shard_map/ppermute | solution.py:15
  16.2 14.3 %collective-permute-start.1 = (f32[16,64]{1,0:T(8,128)}, f32[16,64]{1,0:T(8,128)S(1)}, u32[]{:S(2)}, u32[]{:S(2)}) collective-permute-start(f32[16,64]{1,0:T(8,128)} %get-tuple-element.11), channel_id=1, source_target_pairs={{1,0},{4,1},{5,4},{8,5},{9,8},{12,9},{13,12},{3,2},{6,3},{7,6},{10... | collective-permute-start | bytes 12296 | tf_op jit(solution)/shard_map/ppermute | solution.py:18
  32.1 46.0 %copy-start.14 = (pred[62]{0:T(512)(128)(4,1)S(1)}, pred[62]{0:T(512)(128)(4,1)}, u32[]{:S(2)}) copy-start(pred[62]{0:T(512)(128)(4,1)} %compare_and_fusion.1) | copy-start | bytes 190
  84.1 5.9 %copy-start.2 = (f32[64,16,64]{2,1,0:T(8,128)S(1)}, f32[64,16,64]{2,1,0:T(8,128)}, u32[]{:S(2)}) copy-start(f32[64,16,64]{2,1,0:T(8,128)} %squeeze.19) | copy-start | bytes 786436
  84.1 5.9 %copy-start.8 = (f32[16,16,64]{2,1,0:T(8,128)S(1)}, f32[16,16,64]{2,1,0:T(8,128)}, u32[]{:S(2)}) copy-start(f32[16,16,64]{2,1,0:T(8,128)} %get-tuple-element.10) | copy-start | bytes 196612
  85.2 5.5 %copy-start.1 = (f32[64,16,64]{2,1,0:T(8,128)S(1)}, f32[64,16,64]{2,1,0:T(8,128)}, u32[]{:S(2)}) copy-start(f32[64,16,64]{2,1,0:T(8,128)} %squeeze.20) | copy-start | bytes 786436
  85.2 5.5 %copy-start.7 = (f32[16,16,64]{2,1,0:T(8,128)S(1)}, f32[16,16,64]{2,1,0:T(8,128)}, u32[]{:S(2)}) copy-start(f32[16,16,64]{2,1,0:T(8,128)} %get-tuple-element.9) | copy-start | bytes 196612
  87.6 3.8 %copy-start = (f32[64,16,64]{2,1,0:T(8,128)S(1)}, f32[64,16,64]{2,1,0:T(8,128)}, u32[]{:S(2)}) copy-start(f32[64,16,64]{2,1,0:T(8,128)} %squeeze.21) | copy-start | bytes 786436
  87.7 3.8 %copy-start.6 = (f32[16,16,64]{2,1,0:T(8,128)S(1)}, f32[16,16,64]{2,1,0:T(8,128)}, u32[]{:S(2)}) copy-start(f32[16,16,64]{2,1,0:T(8,128)} %get-tuple-element.8) | copy-start | bytes 196612
Sparse Core Ops, SparseCore 0:
  13.3 31.7 all-gather.1
where the time goes:
time: 101 us; the launch traced here: 99.8 us
  local copies, waits for them, and re-layouts  28.7 us (28%)
  matrix products  20.6 us (20%)
  blocking collectives  19.3 us (19%)
  between operations  13.8 us (14%)
  waiting for transfers between devices  9.48 us (9%)
  other arithmetic  4.24 us (4%)
  starting transfers between devices  3.64 us (4%)
    psum x1, blocking collectives, on_device(): top_field = lax.psum(partial_top, 'branch')  19.3 us
    all_gather x1, waiting for transfers between devices, on_device(): lax.all_gather(coef_table, ('branch', 'inner'), axis=0, tiled=True)  9.46 us
    dot_general x1, matrix products, on_device(): coupled = jnp.einsum('aqb,qcb->qca', slot_blocks, picked, precision=EXACT)  5.97 us
    squeeze x3, local copies, waits for them, and re-layouts, on_device(): stencil[offset]  5.66 us
    gather x1, local copies, waits for them, and re-layouts, on_device(): picked = jnp.take(gathered, row_ids.reshape(-1), axis=0)  3.09 us
    dot_general x4, matrix products, on_device(): jnp.einsum('aqb,qcb->qca', moving, jnp.repeat(fields, 2, axis=0), precisi...  2.92 us
    ppermute x1, starting transfers between devices, with_halo(): lax.ppermute(lax.slice_in_dim(block, block.shape[dim] - width, None, axis...  2.34 us
    dot_general x3, matrix products, on_device(): jnp.einsum('jti,ctj->cti', stencil[offset], extended[:, offset:offset + l...  2.17 us
  transfers between devices with their start and end apart: 3, of which 1 were waited for; matrix products, arithmetic and copies ran while one was open for 19% of the time, Pallas kernels for 0%

commit v1 on v0

v1 whole, which is shorter than its diff:
```python
import functools

import jax
import jax.numpy as jnp
from jax import lax
from jax.experimental import pallas as pl
from jax.experimental.pallas import tpu as pltpu
from jax.sharding import PartitionSpec as P

MESH = pl.DeviceIdType.MESH
NN = (((1,), (0,)), ((), ()))
NT = (((1,), (1,)), ((), ()))


def split(x):
    high = x.astype(jnp.bfloat16)
    return high, (x - high.astype(jnp.float32)).astype(jnp.bfloat16)


def product(x, weights, form):
    rows = x.shape[0]
    high, low = split(x)
    both = jnp.concatenate([high, low], axis=0)
    first = lax.dot_general(both, weights[0], form, preferred_element_type=jnp.float32)
    second = lax.dot_general(high, weights[1], form, preferred_element_type=jnp.float32)
    return first[:rows] + (first[rows:] + second)


def kernel(
    nb, ni,
    vec_hbm, basis_hbm, near_hbm, trans_hbm, coup_hbm, top_hbm, upper_hbm,
    source_ref, target_ref, top_source_ref,
    out_ref,
    vec, basis, near, trans, coup, top, upper,
    halo_low, halo_high, tab_low, tab_self, tab_high, dup, roots, near_sum,
    basis_w, quad_w,
    local_sem, halo_send, halo_recv, leaf_send, leaf_recv, rest_send, rest_recv,
    root_send, root_recv, upper_send, upper_recv,
):
    cols, points = vec.shape
    rank = basis.shape[0]
    assert rank == 64 and near.shape[1] == 64
    wide = 2 * rank
    leaves = points // 64
    levels = leaves.bit_length() - 1
    starts = [2 * leaves - 2 * (leaves >> h) for h in range(levels + 1)]
    clusters = 2 * leaves - 1
    tiles = leaves
    half = leaves // 2
    slots = upper.shape[2] // rank
    n = nb * ni
    branch = lax.axis_index("branch")
    inner = lax.axis_index("inner")
    me = branch * ni + inner

    def place(index):
        return {"branch": index // ni, "inner": index % ni}

    loads = [
        pltpu.make_async_copy(vec_hbm, vec, local_sem.at[0]),
        pltpu.make_async_copy(basis_hbm, basis, local_sem.at[1]),
        pltpu.make_async_copy(upper_hbm, upper.at[branch, 0:rank], local_sem.at[2]),
        pltpu.make_async_copy(trans_hbm, trans, local_sem.at[3]),
        pltpu.make_async_copy(near_hbm, near, local_sem.at[4]),
        pltpu.make_async_copy(coup_hbm, coup, local_sem.at[5]),
        pltpu.make_async_copy(top_hbm, top, local_sem.at[6]),
    ]
    for load in loads:
        load.start()

    barrier = pltpu.get_barrier_semaphore()
    for step in range(1, n):
        pl.semaphore_signal(
            barrier, inc=1, device_id=place((me + step) % n), device_id_type=MESH
        )

    row = lax.broadcasted_iota(jnp.int32, (8, slots * rank), 0)
    lane = lax.broadcasted_iota(jnp.int32, (8, slots * rank), 1)
    meta = jnp.zeros((8, slots * rank), jnp.int32)
    for slot in range(slots):
        here = lane // rank == slot
        meta = jnp.where(here & (row == 0), target_ref[slot], meta)
        meta = jnp.where(here & (row == 1), top_source_ref[slot], meta)
    upper[branch, rank:, :] = meta.astype(jnp.float32)

    def to_high(source, target, send, recv):
        return pltpu.make_async_remote_copy(
            source, target, send.at[0], recv.at[0], device_id=place(me + 1), device_id_type=MESH
        )

    def to_low(source, target, send, recv):
        return pltpu.make_async_remote_copy(
            source, target, send.at[1], recv.at[1], device_id=place(me - 1), device_id_type=MESH
        )

    halo_copies = (
        to_high(vec.at[:, points - wide : points], halo_low, halo_send, halo_recv),
        to_low(vec.at[:, 0:wide], halo_high, halo_send, halo_recv),
    )
    leaf_copies = (
        to_high(tab_self.at[0:half], tab_low.at[0:half], leaf_send, leaf_recv),
        to_low(tab_self.at[0:half], tab_high.at[0:half], leaf_send, leaf_recv),
    )
    rest_copies = (
        to_high(tab_self.at[half:tiles], tab_low.at[half:tiles], rest_send, rest_recv),
        to_low(tab_self.at[half:tiles], tab_high.at[half:tiles], rest_send, rest_recv),
    )
    upper_copies = [
        pltpu.make_async_remote_copy(
            upper.at[branch], upper.at[branch], upper_send.at[step], upper_recv.at[step],
            device_id={"branch": (branch + step) % nb}, device_id_type=MESH,
        )
        for step in range(1, nb)
    ]
    root_copies = [
        pltpu.make_async_remote_copy(
            roots.at[me], roots.at[me], root_send.at[step], root_recv.at[step],
            device_id=place((me + step) % n), device_id_type=MESH,
        )
        for step in range(1, n)
    ]
    has_low = me > 0
    has_high = me < n - 1

    def start(copies):
        @pl.when(has_high)
        def _():
            copies[0].start()

        @pl.when(has_low)
        def _():
            copies[1].start()

    def arrived(copies):
        @pl.when(has_low)
        def _():
            copies[0].wait_recv()

        @pl.when(has_high)
        def _():
            copies[1].wait_recv()

    def sent(copies):
        @pl.when(has_high)
        def _():
            copies[0].wait_send()

        @pl.when(has_low)
        def _():
            copies[1].wait_send()

    low_64 = lax.broadcasted_iota(jnp.int32, (rank, wide), 1) < rank
    low_c = lax.broadcasted_iota(jnp.int32, (cols, wide), 1) < rank
    low_s = lax.broadcasted_iota(jnp.int32, (rank, 2 * wide), 1) < wide

    loads[0].wait()
    loads[1].wait()
    pairs = []
    for k in range(half):
        both = basis[:, k * wide : (k + 1) * wide]
        weights = split(
            jnp.concatenate([jnp.where(low_64, both, 0.0), jnp.where(low_64, 0.0, both)], axis=0)
        )
        basis_w[0, k] = weights[0]
        basis_w[1, k] = weights[1]
        pair = product(vec[:, k * wide : (k + 1) * wide], weights, NT)
        tab_self[k] = pair
        pairs.append(pair)

    pl.semaphore_wait(barrier, n - 1)
    start(halo_copies)
    start(leaf_copies)
    loads[2].wait()
    for copy in upper_copies:
        copy.start()

    loads[3].wait()
    quad = 0
    for h in range(levels - 1):
        breadth = leaves >> h
        base = starts[h] // 2
        lifted = []
        for j in range(breadth // 4):
            at = (base + 2 * j) * wide
            first = trans[:, at : at + wide]
            second = trans[:, at + wide : at + 2 * wide]
            weights = split(
                jnp.concatenate(
                    [
                        jnp.where(low_64, first, 0.0),
                        jnp.where(low_64, pltpu.roll(first, rank, 1), 0.0),
                        jnp.where(low_64, 0.0, pltpu.roll(second, rank, 1)),
                        jnp.where(low_64, 0.0, second),
                    ],
                    axis=0,
                )
            )
            quad_w[0, quad] = weights[0]
            quad_w[1, quad] = weights[1]
            quad += 1
            pair = product(
                jnp.concatenate([pairs[2 * j], pairs[2 * j + 1]], axis=1), weights, NN
            )
            tab_self[starts[h + 1] // 2 + j] = pair
            lifted.append(pair)
        pairs = lifted
    at = starts[levels - 1] * rank
    both = trans[:, at : at + wide]
    last_w = split(
        jnp.concatenate(
            [jnp.where(low_64, both, 0.0), jnp.where(low_64, pltpu.roll(both, rank, 1), 0.0)],
            axis=0,
        )
    )
    single = product(pairs[0], last_w, NN)
    tab_self[tiles - 1] = single
    root = trans[:, (clusters - 1) * rank : clusters * rank]
    root = jnp.concatenate([root, root], axis=1)
    root_w = split(jnp.concatenate([root, root], axis=0))
    roots[me] = product(single, root_w, NN)
    for copy in root_copies:
        copy.start()
    start(rest_copies)

    loads[4].wait()
    arrived(halo_copies)
    turned = [pltpu.roll(vec[:, k * wide : (k + 1) * wide], rank, 1) for k in range(half)]
    before = jnp.where(has_low, pltpu.roll(halo_low[...], rank, 1), 0.0)
    after = jnp.where(has_high, pltpu.roll(halo_high[...], rank, 1), 0.0)
    turned = [before] + turned + [after]
    shifted = [jnp.where(low_c, turned[k], turned[k + 1]) for k in range(half + 1)]
    for k in range(half):
        lanes = slice(k * wide, (k + 1) * wide)
        lower, middle, higher = near[0, :, lanes], near[1, :, lanes], near[2, :, lanes]
        weights = split(
            jnp.concatenate(
                [
                    jnp.where(low_64, lower, 0.0),
                    jnp.where(low_64, middle, lower),
                    jnp.where(low_64, higher, middle),
                    jnp.where(low_64, 0.0, higher),
                ],
                axis=0,
            )
        )
        near_sum[:, lanes] = product(
            jnp.concatenate([shifted[k], shifted[k + 1]], axis=1), weights, NN
        )

    def both_ways(table, offset):
        for k in range(tiles):
            tile = table[k]
            dup[offset + 2 * k] = tile
            dup[offset + 2 * k + 1] = pltpu.roll(tile, rank, 1)

    both_ways(tab_self, 2 * tiles)
    arrived(leaf_copies)
    arrived(rest_copies)

    @pl.when(has_low)
    def _():
        both_ways(tab_low, 0)

    @pl.when(has_high)
    def _():
        both_ways(tab_high, 4 * tiles)

    loads[5].wait()

    def gathered(q):
        h = max(i for i in range(levels + 1) if starts[i] <= q)
        shift = levels - h

        def entry(slot):
            c = source_ref[q, slot]
            run = lax.shift_right_logical(c, shift)
            side = jnp.clip(run - me + 1, 0, 2)
            return side * (2 * tiles) + starts[h] + (c - lax.shift_left(run, shift))

        second = entry(1)
        second = second + 1 - 2 * (second & 1)
        return jnp.where(low_c, dup[entry(0)], dup[second])

    coupled = []
    for k in range(tiles - 1):
        both = coup[:, 2 * k * wide : 2 * (k + 1) * wide]
        weights = split(
            jnp.concatenate([jnp.where(low_s, both, 0.0), jnp.where(low_s, 0.0, both)], axis=0)
        )
        x = jnp.concatenate([gathered(2 * k), gathered(2 * k + 1)], axis=1)
        coupled.append(product(x, weights, NT))
    one = coup[:, (clusters - 1) * wide : clusters * wide]
    coupled.append(
        product(gathered(clusters - 1), split(jnp.concatenate([one, one], axis=0)), NT)
    )

    loads[6].wait()
    top_w = []
    for k in range(nb // 2):
        both = top[:, k * wide : (k + 1) * wide]
        other = pltpu.roll(both, rank, 1)
        top_w.append(
            split(
                jnp.concatenate(
                    [jnp.where(low_64, both, other), jnp.where(low_64, other, both)], axis=0
                )
            )
        )
    own = top[:, pl.ds(pl.multiple_of((branch // 2) * wide, wide), wide)]
    own_w = split(jnp.concatenate([own, own], axis=0))
    for copy in upper_copies:
        copy.wait_recv()
    upper_w = []
    for s in range(nb):
        block = upper[s, 0:rank, :]
        upper_w.append(split(jnp.concatenate([block, block], axis=0)))
    for copy in root_copies:
        copy.wait_recv()
    xu = []
    for g in range(nb):
        total = roots[g * ni]
        for i in range(1, ni):
            total = total + roots[g * ni + i]
        xu.append(total)
    for k in range(nb // 2):
        xu.append(product(jnp.where(low_c, xu[2 * k], xu[2 * k + 1]), top_w[k], NN))
    xu = [jnp.concatenate([x] * (slots * rank // wide), axis=1) for x in xu]
    field = jnp.zeros((2 * cols, wide), jnp.float32)
    first_id = branch.astype(jnp.float32)
    second_id = (nb + branch // 2).astype(jnp.float32)
    for s in range(nb):
        target = upper[s, rank : rank + 1, :]
        source = upper[s, rank + 1 : rank + 2, :]
        chosen = jnp.zeros((cols, slots * rank), jnp.float32)
        for k, x in enumerate(xu):
            chosen = jnp.where(source == float(k), x, chosen)
        x = jnp.concatenate(
            [
                jnp.where(target == first_id, chosen, 0.0),
                jnp.where(target == second_id, chosen, 0.0),
            ],
            axis=0,
        )
        field = field + product(x, upper_w[s], NT)
    side = lax.broadcasted_iota(jnp.int32, (cols, wide), 1) // rank == branch % 2
    own_field = field[:cols] + product(jnp.where(side, field[cols:], 0.0), own_w, NT)

    state = coupled[tiles - 1] + product(jnp.where(low_c, own_field, 0.0), root_w, NT)
    pairs = [coupled[starts[levels - 1] // 2] + product(state, last_w, NT)]
    for h in reversed(range(levels - 1)):
        count = (leaves >> h) // 4
        quad -= count
        base = starts[h] // 2
        lowered = []
        for j in range(count):
            moved = product(pairs[j], (quad_w[0, quad + j], quad_w[1, quad + j]), NT)
            lowered.append(coupled[base + 2 * j] + moved[:, :wide])
            lowered.append(coupled[base + 2 * j + 1] + moved[:, wide:])
        pairs = lowered
    for k in range(half):
        lanes = slice(k * wide, (k + 1) * wide)
        out_ref[:, lanes] = near_sum[:, lanes] + product(
            pairs[k], (basis_w[0, k], basis_w[1, k]), NN
        )

    sent(halo_copies)
    sent(leaf_copies)
    sent(rest_copies)
    for copy in upper_copies + root_copies:
        copy.wait_send()


def on_device(
    vectors,
    leaf_basis,
    near_blocks,
    transfer,
    coupling,
    coupling_source,
    top_transfer,
    upper_coupling_matrices,
    top_target,
    top_source,
):
    cols, points = vectors.shape
    rank = leaf_basis.shape[0]
    leaf_len = near_blocks.shape[1]
    leaves = points // leaf_len
    nb = lax.axis_size("branch")
    ni = lax.axis_size("inner")
    n = nb * ni
    quads = sum((leaves >> h) // 4 for h in range(leaves.bit_length() - 2))
    wide = 2 * rank
    f32, bf16 = jnp.float32, jnp.bfloat16
    dma = pltpu.SemaphoreType.DMA
    hbm = pl.BlockSpec(memory_space=pl.ANY)
    smem = pl.BlockSpec(memory_space=pltpu.SMEM)
    table = pltpu.VMEM((leaves, cols, wide), f32)
    halo = pltpu.VMEM((cols, wide), f32)
    return pl.pallas_call(
        functools.partial(kernel, nb, ni),
        out_shape=jax.ShapeDtypeStruct((cols, points), f32),
        in_specs=[hbm] * 7 + [smem] * 3,
        out_specs=pl.BlockSpec(memory_space=pltpu.VMEM),
        scratch_shapes=[
            pltpu.VMEM(vectors.shape, f32),
            pltpu.VMEM(leaf_basis.shape, f32),
            pltpu.VMEM(near_blocks.shape, f32),
            pltpu.VMEM(transfer.shape, f32),
            pltpu.VMEM(coupling.shape, f32),
            pltpu.VMEM(top_transfer.shape, f32),
            pltpu.VMEM((nb, rank + 8, upper_coupling_matrices.shape[1]), f32),
            halo,
            halo,
            table,
            table,
            table,
            pltpu.VMEM((6 * leaves, cols, wide), f32),
            pltpu.VMEM((n, cols, wide), f32),
            pltpu.VMEM((cols, points), f32),
            pltpu.VMEM((2, leaves // 2, wide, wide), bf16),
            pltpu.VMEM((2, quads, 2 * wide, wide), bf16),
            dma((7,)),
            dma((2,)),
            dma((2,)),
            dma((2,)),
            dma((2,)),
            dma((2,)),
            dma((2,)),
            dma((n,)),
            dma((n,)),
            dma((nb,)),
            dma((nb,)),
        ],
        compiler_params=pltpu.CompilerParams(
            collective_id=0, has_side_effects=True, vmem_limit_bytes=32 * 1024 * 1024
        ),
    )(
        vectors,
        leaf_basis,
        near_blocks,
        transfer,
        coupling,
        top_transfer,
        upper_coupling_matrices,
        coupling_source,
        top_target,
        top_source,
    )


def solution(mesh):
    placed = (
        P("rhs", ("groups", "branch", "inner")),
        P(None, ("groups", "branch", "inner")),
        P(None, None, ("groups", "branch", "inner")),
        P(None, ("groups", "branch", "inner")),
        P(None, ("groups", "branch", "inner")),
        P(("groups", "branch", "inner"), None),
        P(None, "groups"),
        P(None, ("groups", "branch")),
        P(("groups", "branch")),
        P(("groups", "branch")),
    )
    return jax.shard_map(
        on_device,
        mesh=mesh,
        in_specs=placed,
        out_specs=P("rhs", ("groups", "branch", "inner")),
        check_vma=False,
    )
```

time: 101 us -> 27.2 us (0.27)
  matrix products: 20.6 us -> 0 us
  local copies, waits for them, and re-layouts: 28.7 us -> 8.29 us
  blocking collectives: 19.3 us -> 0 us
  Pallas kernels: 0 us -> 18.4 us
  between operations: 13.8 us -> 0.02 us
  waiting for transfers between devices: 9.48 us -> 0 us
  other arithmetic: 4.24 us -> 0 us
  starting transfers between devices: 3.64 us -> 0 us
    dot_general x20 -> x0, matrix products: 20.6 us -> none  [the longest x1 5.97 us: on_device(): coupled = jnp.einsum('aqb,qcb->qca', slot_blocks, picked, precision=EXACT)]
    psum x1 -> x0, blocking collectives: 19.3 us -> none  [on_device(): top_field = lax.psum(partial_top, 'branch')]
    pallas_call x0 -> x1, Pallas kernels: none -> 18.4 us  [on_device(): pl.pallas_call(functools.partial(kernel, nb, ni), out_shape=jax.ShapeDtyp...]
    all_gather x1 -> x0, waiting for transfers between devices: 9.46 us -> none  [on_device(): lax.all_gather(coef_table, ('branch', 'inner'), axis=0, tiled=True)]
    reshape x10 -> x0, local copies, waits for them, and re-layouts: 9.03 us -> none  [the longest x1 2.13 us: on_device(): coupling.reshape(rank_dim, clusters * partner_clusters, rank_dim)]
    unnamed x39 -> x20, local copies, waits for them, and re-layouts: 0.81 us -> 8.29 us
    slice x12 -> x0, local copies, waits for them, and re-layouts: 6.26 us -> none  [the longest x1 1.97 us: on_device(): extended[:, offset:offset + leaves]]
    squeeze x3 -> x0, local copies, waits for them, and re-layouts: 5.66 us -> none  [on_device(): stencil[offset]]
  transfers between devices with their start and end apart: 3 -> 0, of which waited for: 1 -> 0; matrix products, arithmetic and copies ran while one was open for 19% -> 0% of each run, Pallas kernels for 0% -> 0%
where the time goes in v1:
time: 27.2 us; the launch traced here: 26.7 us
  Pallas kernels  18.4 us (68%)
  local copies, waits for them, and re-layouts  8.29 us (30%)
    pallas_call x1, Pallas kernels, on_device(): pl.pallas_call(functools.partial(kernel, nb, ni), out_shape=jax.ShapeDtyp...  18.4 us
    unnamed x20, local copies, waits for them, and re-layouts  8.29 us

profile of v1, /device:TPU:0, one launch (start us, length us, event | category | flops | bytes accessed | tf_op | source)
XLA Modules:
  0.0 26.7 jit_solution(12887099484404444597)
XLA Ops:
  0.0 0.0 copy-start.8
  0.0 0.0 copy-start.7
  0.0 0.8 %copy.11.source_ref = s32[31,2]{1,0:T(8,128)S(1)} copy(s32[31,2]{0,1:T(2,128)} %param.15) | data formatting | bytes 496 | tf_op args[5]
  0.8 0.0 copy-done.8
  0.8 0.0 copy-done.7
  0.8 0.0 copy-start
  0.8 1.2 %copy-done = f32[64,3968]{1,0:T(8,128)S(1)} copy-done((f32[64,3968]{1,0:T(8,128)S(1)}, f32[64,3968]{1,0:T(8,128)}, u32[]{:S(2)}) %copy-start) | copy-done | bytes 1015832
  2.0 0.0 copy-start.1
  2.0 1.1 %copy-done.1 = f32[3,64,1024]{2,1,0:T(8,128)S(1)} copy-done((f32[3,64,1024]{2,1,0:T(8,128)S(1)}, f32[3,64,1024]{2,1,0:T(8,128)}, u32[]{:S(2)}) %copy-start.1) | copy-done | bytes 786456
  3.2 0.0 copy-start.2
  3.2 1.0 %copy-done.2 = f32[64,1984]{1,0:T(8,128)S(1)} copy-done((f32[64,1984]{1,0:T(8,128)S(1)}, f32[64,1984]{1,0:T(8,128)}, u32[]{:S(2)}) %copy-start.2) | copy-done | bytes 507928
  4.2 0.0 copy-start.3
  4.2 0.9 %copy-done.3 = f32[64,1024]{1,0:T(8,128)S(1)} copy-done((f32[64,1024]{1,0:T(8,128)S(1)}, f32[64,1024]{1,0:T(8,128)}, u32[]{:S(2)}) %copy-start.3) | copy-done | bytes 262168
  5.1 0.0 copy-start.4
  5.2 0.8 %copy-done.4 = f32[16,1024]{1,0:T(8,128)S(1)} copy-done((f32[16,1024]{1,0:T(8,128)S(1)}, f32[16,1024]{1,0:T(8,128)}, u32[]{:S(2)}) %copy-start.4) | copy-done | bytes 65560
  6.0 0.0 copy-start.5
  6.0 0.8 %copy-done.5 = f32[64,256]{1,0:T(8,128)S(1)} copy-done((f32[64,256]{1,0:T(8,128)S(1)}, f32[64,256]{1,0:T(8,128)}, u32[]{:S(2)}) %copy-start.5) | copy-done | bytes 65560
  6.8 0.0 copy-start.6
  6.8 0.8 %copy-done.6 = f32[64,256]{1,0:T(8,128)S(1)} copy-done((f32[64,256]{1,0:T(8,128)S(1)}, f32[64,256]{1,0:T(8,128)}, u32[]{:S(2)}) %copy-start.6) | copy-done | bytes 65560
  7.7 18.4 %shard_map.100 = f32[16,1024]{1,0:T(8,128)S(1)} custom-call(f32[16,1024]{1,0:T(8,128)S(1)} %copy-done.4, f32[64,1024]{1,0:T(8,128)S(1)} %copy-done.3, f32[3,64,1024]{2,1,0:T(8,128)S(1)} %copy-done.1, f32[64,1984]{1,0:T(8,128)S(1)} %copy-done.2, f32[64,3968]{1,0:T(8,128)S(1)} %copy-done, f32[64,256]{1,0:T(8,128)S(1)} %copy-done.5, f32[64,256]{1,0:T(8,128)S(1)} %copy-done.6, ...), custom_call_target="tpu_custom_call" | custom-call | tf_op jit(solution)/shard_map/pallas_call | solution.py:400
  26.1 0.6 %copy.13 = f32[16,1024]{1,0:T(8,128)} copy(f32[16,1024]{1,0:T(8,128)S(1)} %shard_map.100) | data formatting | bytes 131072
Async XLA Ops:
  0.0 0.8 %copy-start.8 = (s32[4]{0:T(128)S(1)}, s32[4]{0:T(128)}, u32[]{:S(2)}) copy-start(s32[4]{0:T(128)} %top_source_ref.1) | copy-start | bytes 52
  0.0 0.8 %copy-start.7 = (s32[4]{0:T(128)S(1)}, s32[4]{0:T(128)}, u32[]{:S(2)}) copy-start(s32[4]{0:T(128)} %target_ref.1) | copy-start | bytes 52
  0.8 1.2 %copy-start = (f32[64,3968]{1,0:T(8,128)S(1)}, f32[64,3968]{1,0:T(8,128)}, u32[]{:S(2)}) copy-start(f32[64,3968]{1,0:T(8,128)} %coup_hbm.1) | copy-start | bytes 3047428
  2.0 1.1 %copy-start.1 = (f32[3,64,1024]{2,1,0:T(8,128)S(1)}, f32[3,64,1024]{2,1,0:T(8,128)}, u32[]{:S(2)}) copy-start(f32[3,64,1024]{2,1,0:T(8,128)} %near_hbm.1) | copy-start | bytes 2359300
  3.2 1.0 %copy-start.2 = (f32[64,1984]{1,0:T(8,128)S(1)}, f32[64,1984]{1,0:T(8,128)}, u32[]{:S(2)}) copy-start(f32[64,1984]{1,0:T(8,128)} %trans_hbm.1) | copy-start | bytes 1523716
  4.2 0.9 %copy-start.3 = (f32[64,1024]{1,0:T(8,128)S(1)}, f32[64,1024]{1,0:T(8,128)}, u32[]{:S(2)}) copy-start(f32[64,1024]{1,0:T(8,128)} %basis_hbm.1) | copy-start | bytes 786436
  5.1 0.8 %copy-start.4 = (f32[16,1024]{1,0:T(8,128)S(1)}, f32[16,1024]{1,0:T(8,128)}, u32[]{:S(2)}) copy-start(f32[16,1024]{1,0:T(8,128)} %vec_hbm.1) | copy-start | bytes 196612
  6.0 0.8 %copy-start.5 = (f32[64,256]{1,0:T(8,128)S(1)}, f32[64,256]{1,0:T(8,128)}, u32[]{:S(2)}) copy-start(f32[64,256]{1,0:T(8,128)} %top_hbm.1) | copy-start | bytes 196612
  6.8 0.8 %copy-start.6 = (f32[64,256]{1,0:T(8,128)S(1)}, f32[64,256]{1,0:T(8,128)}, u32[]{:S(2)}) copy-start(f32[64,256]{1,0:T(8,128)} %upper_hbm.1) | copy-start | bytes 196612

commit v2 on v1

--- a/solution.py
+++ b/solution.py
@@ -272,7 +272,7 @@
         shift = levels - h
 
         def entry(slot):
-            c = source_ref[q, slot]
+            c = source_ref[slot, q]
             run = lax.shift_right_logical(c, shift)
             side = jnp.clip(run - me + 1, 0, 2)
             return side * (2 * tiles) + starts[h] + (c - lax.shift_left(run, shift))
@@ -393,7 +393,7 @@
     wide = 2 * rank
     f32, bf16 = jnp.float32, jnp.bfloat16
     dma = pltpu.SemaphoreType.DMA
-    hbm = pl.BlockSpec(memory_space=pl.ANY)
+    hbm = pl.BlockSpec(memory_space=pltpu.HBM)
     smem = pl.BlockSpec(memory_space=pltpu.SMEM)
     table = pltpu.VMEM((leaves, cols, wide), f32)
     halo = pltpu.VMEM((cols, wide), f32)
@@ -433,7 +433,7 @@
             dma((nb,)),
         ],
         compiler_params=pltpu.CompilerParams(
-            collective_id=0, has_side_effects=True, vmem_limit_bytes=32 * 1024 * 1024
+            collective_id=0, has_side_effects=True, vmem_limit_bytes=60 * 1024 * 1024
         ),
     )(
         vectors,
@@ -443,7 +443,7 @@
         coupling,
         top_transfer,
         upper_coupling_matrices,
-        coupling_source,
+        coupling_source.T,
         top_target,
         top_source,
     )

time: 27.2 us -> 20.1 us (0.74)
  local copies, waits for them, and re-layouts: 8.29 us -> 1.47 us
    unnamed x20 -> x1, local copies, waits for them, and re-layouts: 8.29 us -> 1.47 us
where the time goes in v2:
time: 20.1 us; the launch traced here: 19.9 us
  Pallas kernels  18.4 us (92%)
  local copies, waits for them, and re-layouts  1.47 us (7%)
    pallas_call x1, Pallas kernels, on_device(): pl.pallas_call(functools.partial(kernel, nb, ni), out_shape=jax.ShapeDtyp...  18.4 us
    unnamed x1, local copies, waits for them, and re-layouts  1.47 us

profile of v2, /device:TPU:0, one launch (start us, length us, event | category | flops | bytes accessed | tf_op | source)
XLA Modules:
  0.0 19.9 jit_solution(13615871930599663360)
XLA Ops:
  0.0 18.4 %shard_map.100 = f32[16,1024]{1,0:T(8,128)} custom-call(f32[16,1024]{1,0:T(8,128)} %vec_hbm.1, f32[64,1024]{1,0:T(8,128)} %basis_hbm.1, f32[3,64,1024]{2,1,0:T(8,128)} %near_hbm.1, f32[64,1984]{1,0:T(8,128)} %trans_hbm.1, f32[64,3968]{1,0:T(8,128)} %coup_hbm.1, f32[64,256]{1,0:T(8,128)} %top_hbm.1, f32[64,256]{1,0:T(8,128)} %upper_hbm.1, s32[2,31]{1,0:T(2,128)} %bitcast.1, ...), custom_call_target="tpu_custom_call" | custom-call | tf_op jit(solution)/shard_map/pallas_call | solution.py:400
  18.4 1.5 %copy.12 = f32[16,1024]{1,0:T(8,128)} copy(f32[16,1024]{1,0:T(8,128)} %shard_map.100) | data formatting | bytes 131072

commit v3 on v1

--- a/solution.py
+++ b/solution.py
@@ -33,9 +33,9 @@
     out_ref,
     vec, basis, near, trans, coup, top, upper,
     halo_low, halo_high, tab_low, tab_self, tab_high, dup, roots, near_sum,
-    basis_w, quad_w,
-    local_sem, halo_send, halo_recv, leaf_send, leaf_recv, rest_send, rest_recv,
-    root_send, root_recv, upper_send, upper_recv,
+    basis_w, quad_w, coup_w, parts, fields,
+    local_sem, halo_send, halo_recv, table_send, table_recv,
+    root_send, root_recv, field_send, field_recv,
 ):
     cols, points = vec.shape
     rank = basis.shape[0]
@@ -47,7 +47,7 @@
     clusters = 2 * leaves - 1
     tiles = leaves
     half = leaves // 2
-    slots = upper.shape[2] // rank
+    slots = upper.shape[1] // rank
     n = nb * ni
     branch = lax.axis_index("branch")
     inner = lax.axis_index("inner")
@@ -59,7 +59,7 @@
     loads = [
         pltpu.make_async_copy(vec_hbm, vec, local_sem.at[0]),
         pltpu.make_async_copy(basis_hbm, basis, local_sem.at[1]),
-        pltpu.make_async_copy(upper_hbm, upper.at[branch, 0:rank], local_sem.at[2]),
+        pltpu.make_async_copy(upper_hbm, upper, local_sem.at[2]),
         pltpu.make_async_copy(trans_hbm, trans, local_sem.at[3]),
         pltpu.make_async_copy(near_hbm, near, local_sem.at[4]),
         pltpu.make_async_copy(coup_hbm, coup, local_sem.at[5]),
@@ -74,15 +74,6 @@
             barrier, inc=1, device_id=place((me + step) % n), device_id_type=MESH
         )
 
-    row = lax.broadcasted_iota(jnp.int32, (8, slots * rank), 0)
-    lane = lax.broadcasted_iota(jnp.int32, (8, slots * rank), 1)
-    meta = jnp.zeros((8, slots * rank), jnp.int32)
-    for slot in range(slots):
-        here = lane // rank == slot
-        meta = jnp.where(here & (row == 0), target_ref[slot], meta)
-        meta = jnp.where(here & (row == 1), top_source_ref[slot], meta)
-    upper[branch, rank:, :] = meta.astype(jnp.float32)
-
     def to_high(source, target, send, recv):
         return pltpu.make_async_remote_copy(
             source, target, send.at[0], recv.at[0], device_id=place(me + 1), device_id_type=MESH
@@ -97,17 +88,14 @@
         to_high(vec.at[:, points - wide : points], halo_low, halo_send, halo_recv),
         to_low(vec.at[:, 0:wide], halo_high, halo_send, halo_recv),
     )
-    leaf_copies = (
-        to_high(tab_self.at[0:half], tab_low.at[0:half], leaf_send, leaf_recv),
-        to_low(tab_self.at[0:half], tab_high.at[0:half], leaf_send, leaf_recv),
-    )
-    rest_copies = (
-        to_high(tab_self.at[half:tiles], tab_low.at[half:tiles], rest_send, rest_recv),
-        to_low(tab_self.at[half:tiles], tab_high.at[half:tiles], rest_send, rest_recv),
-    )
-    upper_copies = [
+    table_copies = (
+        to_high(tab_self, tab_low, table_send, table_recv),
+        to_low(tab_self, tab_high, table_send, table_recv),
+    )
+    field_copies = [
         pltpu.make_async_remote_copy(
-            upper.at[branch], upper.at[branch], upper_send.at[step], upper_recv.at[step],
+            parts.at[(branch + step) % nb], fields.at[branch],
+            field_send.at[step], field_recv.at[step],
             device_id={"branch": (branch + step) % nb}, device_id_type=MESH,
         )
         for step in range(1, nb)
@@ -166,13 +154,6 @@
         pair = product(vec[:, k * wide : (k + 1) * wide], weights, NT)
         tab_self[k] = pair
         pairs.append(pair)
-
-    pl.semaphore_wait(barrier, n - 1)
-    start(halo_copies)
-    start(leaf_copies)
-    loads[2].wait()
-    for copy in upper_copies:
-        copy.start()
 
     loads[3].wait()
     quad = 0
@@ -218,18 +199,9 @@
     root = jnp.concatenate([root, root], axis=1)
     root_w = split(jnp.concatenate([root, root], axis=0))
     roots[me] = product(single, root_w, NN)
-    for copy in root_copies:
-        copy.start()
-    start(rest_copies)
-
-    loads[4].wait()
-    arrived(halo_copies)
     turned = [pltpu.roll(vec[:, k * wide : (k + 1) * wide], rank, 1) for k in range(half)]
-    before = jnp.where(has_low, pltpu.roll(halo_low[...], rank, 1), 0.0)
-    after = jnp.where(has_high, pltpu.roll(halo_high[...], rank, 1), 0.0)
-    turned = [before] + turned + [after]
-    shifted = [jnp.where(low_c, turned[k], turned[k + 1]) for k in range(half + 1)]
-    for k in range(half):
+
+    def dense(k, first, second):
         lanes = slice(k * wide, (k + 1) * wide)
         lower, middle, higher = near[0, :, lanes], near[1, :, lanes], near[2, :, lanes]
         weights = split(
@@ -243,9 +215,12 @@
                 axis=0,
             )
         )
-        near_sum[:, lanes] = product(
-            jnp.concatenate([shifted[k], shifted[k + 1]], axis=1), weights, NN
-        )
+        near_sum[:, lanes] = product(jnp.concatenate([first, second], axis=1), weights, NN)
+
+    shifted = [jnp.where(low_c, turned[k], turned[k + 1]) for k in range(half - 1)]
+    loads[4].wait()
+    for k in range(1, half - 1):
+        dense(k, shifted[k - 1], shifted[k])
 
     def both_ways(table, offset):
         for k in range(tiles):
@@ -254,46 +229,17 @@
             dup[offset + 2 * k + 1] = pltpu.roll(tile, rank, 1)
 
     both_ways(tab_self, 2 * tiles)
-    arrived(leaf_copies)
-    arrived(rest_copies)
-
-    @pl.when(has_low)
-    def _():
-        both_ways(tab_low, 0)
-
-    @pl.when(has_high)
-    def _():
-        both_ways(tab_high, 4 * tiles)
-
     loads[5].wait()
-
-    def gathered(q):
-        h = max(i for i in range(levels + 1) if starts[i] <= q)
-        shift = levels - h
-
-        def entry(slot):
-            c = source_ref[q, slot]
-            run = lax.shift_right_logical(c, shift)
-            side = jnp.clip(run - me + 1, 0, 2)
-            return side * (2 * tiles) + starts[h] + (c - lax.shift_left(run, shift))
-
-        second = entry(1)
-        second = second + 1 - 2 * (second & 1)
-        return jnp.where(low_c, dup[entry(0)], dup[second])
-
-    coupled = []
     for k in range(tiles - 1):
         both = coup[:, 2 * k * wide : 2 * (k + 1) * wide]
         weights = split(
             jnp.concatenate([jnp.where(low_s, both, 0.0), jnp.where(low_s, 0.0, both)], axis=0)
         )
-        x = jnp.concatenate([gathered(2 * k), gathered(2 * k + 1)], axis=1)
-        coupled.append(product(x, weights, NT))
+        coup_w[0, k] = weights[0]
+        coup_w[1, k] = weights[1]
     one = coup[:, (clusters - 1) * wide : clusters * wide]
-    coupled.append(
-        product(gathered(clusters - 1), split(jnp.concatenate([one, one], axis=0)), NT)
-    )
-
+    one_w = split(jnp.concatenate([one, one], axis=0))
+    loads[2].wait()
     loads[6].wait()
     top_w = []
     for k in range(nb // 2):
@@ -308,12 +254,21 @@
         )
     own = top[:, pl.ds(pl.multiple_of((branch // 2) * wide, wide), wide)]
     own_w = split(jnp.concatenate([own, own], axis=0))
-    for copy in upper_copies:
-        copy.wait_recv()
-    upper_w = []
-    for s in range(nb):
-        block = upper[s, 0:rank, :]
-        upper_w.append(split(jnp.concatenate([block, block], axis=0)))
+    block = upper[...]
+    upper_w = split(jnp.concatenate([block, block], axis=0))
+    lane = lax.broadcasted_iota(jnp.int32, (cols, slots * rank), 1) // rank
+    target = jnp.zeros((cols, slots * rank), jnp.int32)
+    source = target
+    for slot in range(slots):
+        target = jnp.where(lane == slot, target_ref[slot], target)
+        source = jnp.where(lane == slot, top_source_ref[slot], source)
+
+    pl.semaphore_wait(barrier, n - 1)
+    for copy in root_copies:
+        copy.start()
+    start(halo_copies)
+    start(table_copies)
+
     for copy in root_copies:
         copy.wait_recv()
     xu = []
@@ -324,26 +279,70 @@
         xu.append(total)
     for k in range(nb // 2):
         xu.append(product(jnp.where(low_c, xu[2 * k], xu[2 * k + 1]), top_w[k], NN))
-    xu = [jnp.concatenate([x] * (slots * rank // wide), axis=1) for x in xu]
-    field = jnp.zeros((2 * cols, wide), jnp.float32)
-    first_id = branch.astype(jnp.float32)
-    second_id = (nb + branch // 2).astype(jnp.float32)
-    for s in range(nb):
-        target = upper[s, rank : rank + 1, :]
-        source = upper[s, rank + 1 : rank + 2, :]
-        chosen = jnp.zeros((cols, slots * rank), jnp.float32)
-        for k, x in enumerate(xu):
-            chosen = jnp.where(source == float(k), x, chosen)
-        x = jnp.concatenate(
-            [
-                jnp.where(target == first_id, chosen, 0.0),
-                jnp.where(target == second_id, chosen, 0.0),
-            ],
-            axis=0,
-        )
-        field = field + product(x, upper_w[s], NT)
-    side = lax.broadcasted_iota(jnp.int32, (cols, wide), 1) // rank == branch % 2
-    own_field = field[:cols] + product(jnp.where(side, field[cols:], 0.0), own_w, NT)
+    chosen = jnp.zeros((cols, slots * rank), jnp.float32)
+    for k, x in enumerate(xu):
+        x = jnp.concatenate([x] * (slots * rank // wide), axis=1)
+        chosen = jnp.where(source == k, x, chosen)
+    field = product(
+        jnp.concatenate(
+            [jnp.where(target == k, chosen, 0.0) for k in range(nb + nb // 2)], axis=0
+        ),
+        upper_w,
+        NT,
+    )
+    for g in range(nb):
+        second = nb + g // 2
+        parts[g] = jnp.where(
+            low_c, field[g * cols : (g + 1) * cols], field[second * cols : (second + 1) * cols]
+        )
+    for copy in field_copies:
+        copy.start()
+
+    arrived(halo_copies)
+    before = jnp.where(has_low, pltpu.roll(halo_low[...], rank, 1), 0.0)
+    after = jnp.where(has_high, pltpu.roll(halo_high[...], rank, 1), 0.0)
+    dense(0, jnp.where(low_c, before, turned[0]), shifted[0])
+    dense(half - 1, shifted[half - 2], jnp.where(low_c, turned[half - 1], after))
+
+    arrived(table_copies)
+
+    @pl.when(has_low)
+    def _():
+        both_ways(tab_low, 0)
+
+    @pl.when(has_high)
+    def _():
+        both_ways(tab_high, 4 * tiles)
+
+    def gathered(q):
+        h = max(i for i in range(levels + 1) if starts[i] <= q)
+        shift = levels - h
+
+        def entry(slot):
+            c = source_ref[slot, q]
+            run = lax.shift_right_logical(c, shift)
+            side = jnp.clip(run - me + 1, 0, 2)
+            return side * (2 * tiles) + starts[h] + (c - lax.shift_left(run, shift))
+
+        second = entry(1)
+        second = second + 1 - 2 * (second & 1)
+        return jnp.where(low_c, dup[entry(0)], dup[second])
+
+    coupled = []
+    for k in range(tiles - 1):
+        x = jnp.concatenate([gathered(2 * k), gathered(2 * k + 1)], axis=1)
+        coupled.append(product(x, (coup_w[0, k], coup_w[1, k]), NT))
+    coupled.append(product(gathered(clusters - 1), one_w, NT))
+
+    own_field = parts[branch]
+    for copy in field_copies:
+        copy.wait_recv()
+    for step in range(1, nb):
+        own_field = own_field + fields[(branch + nb - step) % nb]
+    odd = branch % 2
+    side = lax.broadcasted_iota(jnp.int32, (cols, wide), 1) // rank == odd
+    upper_part = jnp.where(odd == 1, own_field, pltpu.roll(own_field, rank, 1))
+    own_field = own_field + product(jnp.where(side, upper_part, 0.0), own_w, NT)
 
     state = coupled[tiles - 1] + product(jnp.where(low_c, own_field, 0.0), root_w, NT)
     pairs = [coupled[starts[levels - 1] // 2] + product(state, last_w, NT)]
@@ -364,9 +363,8 @@
         )
 
     sent(halo_copies)
-    sent(leaf_copies)
-    sent(rest_copies)
-    for copy in upper_copies + root_copies:
+    sent(table_copies)
+    for copy in field_copies + root_copies:
         copy.wait_send()
 
 
@@ -393,7 +391,7 @@
     wide = 2 * rank
     f32, bf16 = jnp.float32, jnp.bfloat16
     dma = pltpu.SemaphoreType.DMA
-    hbm = pl.BlockSpec(memory_space=pl.ANY)
+    hbm = pl.BlockSpec(memory_space=pltpu.HBM)
     smem = pl.BlockSpec(memory_space=pltpu.SMEM)
     table = pltpu.VMEM((leaves, cols, wide), f32)
     halo = pltpu.VMEM((cols, wide), f32)
@@ -409,7 +407,7 @@
             pltpu.VMEM(transfer.shape, f32),
             pltpu.VMEM(coupling.shape, f32),
             pltpu.VMEM(top_transfer.shape, f32),
-            pltpu.VMEM((nb, rank + 8, upper_coupling_matrices.shape[1]), f32),
+            pltpu.VMEM(upper_coupling_matrices.shape, f32),
             halo,
             halo,
             table,
@@ -420,9 +418,10 @@
             pltpu.VMEM((cols, points), f32),
             pltpu.VMEM((2, leaves // 2, wide, wide), bf16),
             pltpu.VMEM((2, quads, 2 * wide, wide), bf16),
+            pltpu.VMEM((2, leaves - 1, wide, 2 * wide), bf16),
+            pltpu.VMEM((nb, cols, wide), f32),
+            pltpu.VMEM((nb, cols, wide), f32),
             dma((7,)),
-            dma((2,)),
-            dma((2,)),
             dma((2,)),
             dma((2,)),
             dma((2,)),
@@ -433,7 +432,7 @@
             dma((nb,)),
         ],
         compiler_params=pltpu.CompilerParams(
-            collective_id=0, has_side_effects=True, vmem_limit_bytes=32 * 1024 * 1024
+            collective_id=0, has_side_effects=True, vmem_limit_bytes=60 * 1024 * 1024
         ),
     )(
         vectors,
@@ -443,7 +442,7 @@
         coupling,
         top_transfer,
         upper_coupling_matrices,
-        coupling_source,
+        coupling_source.T,
         top_target,
         top_source,
     )

time: 27.2 us -> 17.8 us (0.65)
  local copies, waits for them, and re-layouts: 8.29 us -> 1.47 us
  Pallas kernels: 18.4 us -> 16.1 us
    unnamed x20 -> x1, local copies, waits for them, and re-layouts: 8.29 us -> 1.47 us
    pallas_call x1, Pallas kernels: 18.4 us -> 16.1 us  [on_device(): pl.pallas_call(functools.partial(kernel, nb, ni), out_shape=jax.ShapeDtyp...]
where the time goes in v3:
time: 17.8 us; the launch traced here: 17.6 us
  Pallas kernels  16.1 us (90%)
  local copies, waits for them, and re-layouts  1.47 us (8%)
    pallas_call x1, Pallas kernels, on_device(): pl.pallas_call(functools.partial(kernel, nb, ni), out_shape=jax.ShapeDtyp...  16.1 us
    unnamed x1, local copies, waits for them, and re-layouts  1.47 us

profile of v3, /device:TPU:0, one launch (start us, length us, event | category | flops | bytes accessed | tf_op | source)
XLA Modules:
  0.0 17.6 jit_solution(12173749056264272480)
XLA Ops:
  0.0 16.1 %shard_map.100 = f32[16,1024]{1,0:T(8,128)} custom-call(f32[16,1024]{1,0:T(8,128)} %vec_hbm.1, f32[64,1024]{1,0:T(8,128)} %basis_hbm.1, f32[3,64,1024]{2,1,0:T(8,128)} %near_hbm.1, f32[64,1984]{1,0:T(8,128)} %trans_hbm.1, f32[64,3968]{1,0:T(8,128)} %coup_hbm.1, f32[64,256]{1,0:T(8,128)} %top_hbm.1, f32[64,256]{1,0:T(8,128)} %upper_hbm.1, s32[2,31]{1,0:T(2,128)} %bitcast.1, ...), custom_call_target="tpu_custom_call" | custom-call | tf_op jit(solution)/shard_map/pallas_call | solution.py:398
  16.1 1.5 %copy.12 = f32[16,1024]{1,0:T(8,128)} copy(f32[16,1024]{1,0:T(8,128)} %shard_map.100) | data formatting | bytes 131072

commit v4 on v3

--- a/solution.py
+++ b/solution.py
@@ -65,14 +65,13 @@
         pltpu.make_async_copy(coup_hbm, coup, local_sem.at[5]),
         pltpu.make_async_copy(top_hbm, top, local_sem.at[6]),
     ]
-    for load in loads:
-        load.start()
-
     barrier = pltpu.get_barrier_semaphore()
     for step in range(1, n):
         pl.semaphore_signal(
             barrier, inc=1, device_id=place((me + step) % n), device_id_type=MESH
         )
+    for load in loads:
+        load.start()
 
     def to_high(source, target, send, recv):
         return pltpu.make_async_remote_copy(
@@ -198,7 +197,10 @@
     root = trans[:, (clusters - 1) * rank : clusters * rank]
     root = jnp.concatenate([root, root], axis=1)
     root_w = split(jnp.concatenate([root, root], axis=0))
-    roots[me] = product(single, root_w, NN)
+    term = product(single, root_w, NN)
+    part = cols // 2
+    low_p = lax.broadcasted_iota(jnp.int32, (part, wide), 1) < rank
+    roots[me] = jnp.where(low_p, term[:part], term[part:])
     turned = [pltpu.roll(vec[:, k * wide : (k + 1) * wide], rank, 1) for k in range(half)]
 
     def dense(k, first, second):
@@ -218,9 +220,6 @@
         near_sum[:, lanes] = product(jnp.concatenate([first, second], axis=1), weights, NN)
 
     shifted = [jnp.where(low_c, turned[k], turned[k + 1]) for k in range(half - 1)]
-    loads[4].wait()
-    for k in range(1, half - 1):
-        dense(k, shifted[k - 1], shifted[k])
 
     def both_ways(table, offset):
         for k in range(tiles):
@@ -276,7 +275,12 @@
         total = roots[g * ni]
         for i in range(1, ni):
             total = total + roots[g * ni + i]
-        xu.append(total)
+        other = pltpu.roll(total, rank, 1)
+        xu.append(
+            jnp.concatenate(
+                [jnp.where(low_p, total, other), jnp.where(low_p, other, total)], axis=0
+            )
+        )
     for k in range(nb // 2):
         xu.append(product(jnp.where(low_c, xu[2 * k], xu[2 * k + 1]), top_w[k], NN))
     chosen = jnp.zeros((cols, slots * rank), jnp.float32)
@@ -298,6 +302,9 @@
     for copy in field_copies:
         copy.start()
 
+    loads[4].wait()
+    for k in range(1, half - 1):
+        dense(k, shifted[k - 1], shifted[k])
     arrived(halo_copies)
     before = jnp.where(has_low, pltpu.roll(halo_low[...], rank, 1), 0.0)
     after = jnp.where(has_high, pltpu.roll(halo_high[...], rank, 1), 0.0)
@@ -414,7 +421,7 @@
             table,
             table,
             pltpu.VMEM((6 * leaves, cols, wide), f32),
-            pltpu.VMEM((n, cols, wide), f32),
+            pltpu.VMEM((n, cols // 2, wide), f32),
             pltpu.VMEM((cols, points), f32),
             pltpu.VMEM((2, leaves // 2, wide, wide), bf16),
             pltpu.VMEM((2, quads, 2 * wide, wide), bf16),

time: 17.8 us -> 17.4 us (0.978)
  Pallas kernels: 16.1 us -> 15.7 us
    pallas_call x1, Pallas kernels: 16.1 us -> 15.7 us  [on_device(): pl.pallas_call(functools.partial(kernel, nb, ni), out_shape=jax.ShapeDtyp...]
where the time goes in v4:
time: 17.4 us; the launch traced here: 17.2 us
  Pallas kernels  15.7 us (90%)
  local copies, waits for them, and re-layouts  1.47 us (8%)
    pallas_call x1, Pallas kernels, on_device(): pl.pallas_call(functools.partial(kernel, nb, ni), out_shape=jax.ShapeDtyp...  15.7 us
    unnamed x1, local copies, waits for them, and re-layouts  1.47 us

profile of v4, /device:TPU:0, one launch (start us, length us, event | category | flops | bytes accessed | tf_op | source)
XLA Modules:
  0.0 17.2 jit_solution(2763205398048092677)
XLA Ops:
  0.0 15.7 %shard_map.100 = f32[16,1024]{1,0:T(8,128)} custom-call(f32[16,1024]{1,0:T(8,128)} %vec_hbm.1, f32[64,1024]{1,0:T(8,128)} %basis_hbm.1, f32[3,64,1024]{2,1,0:T(8,128)} %near_hbm.1, f32[64,1984]{1,0:T(8,128)} %trans_hbm.1, f32[64,3968]{1,0:T(8,128)} %coup_hbm.1, f32[64,256]{1,0:T(8,128)} %top_hbm.1, f32[64,256]{1,0:T(8,128)} %upper_hbm.1, s32[2,31]{1,0:T(2,128)} %bitcast.1, ...), custom_call_target="tpu_custom_call" | custom-call | tf_op jit(solution)/shard_map/pallas_call | solution.py:405
  15.7 1.5 %copy.12 = f32[16,1024]{1,0:T(8,128)} copy(f32[16,1024]{1,0:T(8,128)} %shard_map.100) | data formatting | bytes 131072
